TPU v7x, 32 devices: a whole 2x2x4 slice. The times are simulated.
32 devices in a mesh: parts: 2 (over y), seq: 4 (over z), dp: 2 (over x), fsdp: 2 (over core).
Axes of the slice: x: 2, y: 2, z: 4, core: 2. Of those that a mesh axis runs over, the one named last changes fastest.
Arguments:
- queries: bfloat16 [8, 512, 2048], P(('parts', 'dp', 'fsdp'), 'seq'), parts along dimension 0, may hold values from -6 to 6
- key_states: bfloat16 [8, 512, 512], P(('parts', 'dp', 'fsdp'), 'seq'), parts along dimension 0, may hold values from -6 to 6
- values: bfloat16 [8, 512, 512], P(('parts', 'dp', 'fsdp'), 'seq'), parts along dimension 0, may hold values from -6 to 6
- grad_out: bfloat16 [8, 512, 2048], P(('parts', 'dp', 'fsdp'), 'seq'), parts along dimension 0, may hold values from -6 to 6
- segments: int32 [8, 512], P(('parts', 'dp', 'fsdp'), 'seq'), parts along dimension 0, may hold values from 0 to 7, never falling along the last dimension, each value on 1 to 256 neighbouring positions
Outputs:
- attended: bfloat16 [8, 512, 2048], P(('parts', 'dp', 'fsdp'), 'seq'), parts along dimension 0
- query_grad: bfloat16 [8, 512, 2048], P(('parts', 'dp', 'fsdp'), 'seq'), parts along dimension 0
- key_grad: bfloat16 [8, 512, 512], P(('parts', 'dp', 'fsdp'), 'seq'), parts along dimension 0
- value_grad: bfloat16 [8, 512, 512], P(('parts', 'dp', 'fsdp'), 'seq'), parts along dimension 0
There are 2 independent parts, one for each index of `parts`. A program takes and returns all parts, laid end to end along the dimension named above; each array names one. Nothing has to cross between parts.
Inputs may be any that keep to these rules, and one draw needn't show every extreme that they name: `segments`: document numbers never fall along a row; every document has 1 to 256 tokens and one of each row has exactly 256.
All inputs are finite; a program needn't handle non-finite values.
Results may differ from a plain program's by a relative error of at most 0.0093.
Values may be sent and summed in bfloat16 or wider, within the bound.
A program may use at most 64 MiB of HBM per device.

v0:
```python
from functools import partial

import jax
import jax.numpy as jnp
from jax import lax
from jax.sharding import PartitionSpec as P

H = 16
KVH = 4
HD = 128


tile_limit = 512
neg_large = -1e30


def product(left, right):
    return jnp.dot(left, right, preferred_element_type=jnp.float32)


def contract(left, right):
    return lax.dot_general(
        left, right, (((1,), (1,)), ((), ())), preferred_element_type=jnp.float32
    )


def transposed(left, right):
    return lax.dot_general(
        left, right, (((0,), (0,)), ((), ())), preferred_element_type=jnp.float32
    )


def keep_same(running):
    return running


def make_tiles(queries, key_states, values, grad_out, segment_ids):
    length, head_width = queries.shape
    tile_rows = min(tile_limit, length)
    tile_count = length // tile_rows
    score_scale = head_width ** (-0.5)
    positions = jnp.arange(length, dtype=jnp.int32)

    def block_of(source, index):
        return lax.dynamic_slice_in_dim(source, index * tile_rows, tile_rows, 0)

    def active(query_block, key_block):
        live = key_block <= query_block
        return live

    def scores_of(query_block, key_block):
        scores = (
            contract(block_of(queries, query_block), block_of(key_states, key_block)) * score_scale
        )
        causal = (
            block_of(positions, query_block)[:, None] >= block_of(positions, key_block)[None, :]
        )
        same_doc = (
            block_of(segment_ids, query_block)[:, None] == block_of(segment_ids, key_block)[None, :]
        )
        return (scores, jnp.logical_and(causal, same_doc))

    def row_stats(query_block):

        def row_advance(key_block, running):

            def row_update(running):
                row_top, row_total = running
                scores, allowed = scores_of(query_block, key_block)
                masked = jnp.where(allowed, scores, neg_large)
                new_top = jnp.maximum(row_top, jnp.max(masked, axis=1))
                exponents = jnp.where(allowed, jnp.exp(masked - new_top[:, None]), 0.0)
                return (
                    new_top,
                    row_total * jnp.exp(row_top - new_top) + jnp.sum(exponents, axis=1),
                )

            return lax.cond(active(query_block, key_block), row_update, keep_same, running)

        initial = (
            jnp.full((tile_rows,), neg_large, jnp.float32),
            jnp.zeros((tile_rows,), jnp.float32),
        )
        return lax.fori_loop(0, tile_count, row_advance, initial)

    def weights_of(query_block, key_block, row_top, row_total):
        scores, allowed = scores_of(query_block, key_block)
        return jnp.where(allowed, jnp.exp(scores - row_top[:, None]), 0.0) / row_total[:, None]

    def output_rows(query_block, row_top, row_total):

        def output_advance(key_block, running):

            def output_update(running):
                weights_low = weights_of(query_block, key_block, row_top, row_total).astype(
                    jnp.bfloat16
                )
                return running + product(weights_low, block_of(values, key_block))

            return lax.cond(active(query_block, key_block), output_update, keep_same, running)

        return lax.fori_loop(
            0, tile_count, output_advance, jnp.zeros((tile_rows, head_width), jnp.float32)
        )

    def grad_rows(query_block, row_top, row_total, out_rows, key_grads, value_grads):
        grad_tile = block_of(grad_out, query_block)
        query_tile = block_of(queries, query_block)
        row_delta = jnp.sum(grad_tile.astype(jnp.float32) * out_rows, axis=1)

        def grad_advance(key_block, running):

            def grad_update(running):
                query_grad, key_grads, value_grads = running
                weights = weights_of(query_block, key_block, row_top, row_total)
                spread = contract(grad_tile, block_of(values, key_block))
                score_grad = (weights * (spread - row_delta[:, None])).astype(jnp.bfloat16)
                query_grad = query_grad + product(score_grad, block_of(key_states, key_block))
                start = key_block * tile_rows
                key_part = (
                    block_of(key_grads, key_block)
                    + transposed(score_grad, query_tile) * score_scale
                )
                value_part = block_of(value_grads, key_block) + transposed(
                    weights.astype(jnp.bfloat16), grad_tile
                )
                key_grads = lax.dynamic_update_slice_in_dim(key_grads, key_part, start, 0)
                value_grads = lax.dynamic_update_slice_in_dim(value_grads, value_part, start, 0)
                return (query_grad, key_grads, value_grads)

            return lax.cond(active(query_block, key_block), grad_update, keep_same, running)

        initial = (jnp.zeros((tile_rows, head_width), jnp.float32), key_grads, value_grads)
        query_grad, key_grads, value_grads = lax.fori_loop(0, tile_count, grad_advance, initial)
        return (query_grad * score_scale, key_grads, value_grads)

    return (tile_count, tile_rows, row_stats, output_rows, grad_rows, block_of)


def joined_unit(documents, inputs):
    queries, key_states, values, grad_out, segment_ids = inputs
    tile_count, tile_rows, row_stats, output_rows, grad_rows, block_of = make_tiles(
        queries, key_states, values, grad_out, segment_ids
    )
    length, head_width = queries.shape

    def joined_advance(query_block, running):
        attended, query_grads, key_grads, value_grads = running
        row_top, row_total = row_stats(query_block)
        out_rows = output_rows(query_block, row_top, row_total)
        query_grad, key_grads, value_grads = grad_rows(
            query_block, row_top, row_total, out_rows, key_grads, value_grads
        )
        start = query_block * tile_rows
        attended = lax.dynamic_update_slice_in_dim(attended, out_rows, start, 0)
        query_grads = lax.dynamic_update_slice_in_dim(query_grads, query_grad, start, 0)
        return (attended, query_grads, key_grads, value_grads)

    zeros_full = jnp.zeros((length, head_width), jnp.float32)
    return lax.fori_loop(
        0, tile_count, joined_advance, (zeros_full, zeros_full, zeros_full, zeros_full)
    )


def local(queries, key_states, values, grad_out, segments):
    batch_rows, local_rows, query_width = queries.shape
    members = lax.axis_size("seq")
    local_heads = H // members
    copies = max(1, members // KVH)
    local_kv = KVH * copies // members
    group_size = local_heads // local_kv
    length = local_rows * members

    def spread_kv(array_in):
        expanded = jnp.repeat(array_in.reshape(batch_rows, local_rows, KVH, HD), copies, axis=2)
        return expanded

    query_split = queries.reshape(batch_rows, local_rows, members, local_heads * HD)
    grad_split = grad_out.reshape(batch_rows, local_rows, members, local_heads * HD)
    query_heads, key_heads, value_heads, grad_heads = (
        lax.all_to_all(query_split, "seq", split_axis=2, concat_axis=1, tiled=True),
        lax.all_to_all(spread_kv(key_states), "seq", split_axis=2, concat_axis=1, tiled=True),
        lax.all_to_all(spread_kv(values), "seq", split_axis=2, concat_axis=1, tiled=True),
        lax.all_to_all(grad_split, "seq", split_axis=2, concat_axis=1, tiled=True),
    )
    segment_row = lax.all_gather(segments, "seq", axis=1, tiled=True)

    def to_units(array_in, head_count):
        return (
            array_in.reshape(batch_rows, length, head_count, HD)
            .transpose(0, 2, 1, 3)
            .reshape(batch_rows * head_count, length, HD)
        )

    def to_rows(array_in, head_count, out_type):
        shaped = array_in.reshape(batch_rows, head_count, length, HD).transpose(0, 2, 1, 3)
        return shaped.reshape(batch_rows, length, 1, head_count * HD).astype(out_type)

    def kv_rows(array_in):
        summed = array_in.reshape(batch_rows, local_kv, group_size, length, HD).sum(axis=2)
        return to_rows(summed, local_kv, jnp.bfloat16)

    key_units = jnp.repeat(key_heads, group_size, axis=2)
    value_units = jnp.repeat(value_heads, group_size, axis=2)
    unit_inputs = (
        to_units(query_heads, local_heads),
        to_units(key_units, local_heads),
        to_units(value_units, local_heads),
        to_units(grad_heads, local_heads),
        jnp.repeat(segment_row, local_heads, axis=0),
    )
    documents = False
    attended, query_grads, key_grads, value_grads = lax.map(
        partial(joined_unit, documents), unit_inputs
    )
    attended_back, query_back = (
        lax.all_to_all(
            to_rows(attended, local_heads, jnp.bfloat16),
            "seq",
            split_axis=1,
            concat_axis=2,
            tiled=True,
        ),
        lax.all_to_all(
            to_rows(query_grads, local_heads, jnp.bfloat16),
            "seq",
            split_axis=1,
            concat_axis=2,
            tiled=True,
        ),
    )
    key_back, value_back = (
        lax.all_to_all(kv_rows(key_grads), "seq", split_axis=1, concat_axis=2, tiled=True),
        lax.all_to_all(kv_rows(value_grads), "seq", split_axis=1, concat_axis=2, tiled=True),
    )

    def finish_kv(array_in):
        summed = (
            array_in.astype(jnp.float32)
            .reshape(batch_rows, local_rows, KVH, copies, HD)
            .sum(axis=3)
        )
        return summed.astype(jnp.bfloat16).reshape(batch_rows, local_rows, KVH * HD)

    attended_out = attended_back.reshape(batch_rows, local_rows, query_width)
    query_out = query_back.reshape(batch_rows, local_rows, query_width)
    return (attended_out, query_out, finish_kv(key_back), finish_kv(value_back))


def solution(mesh):
    in_specs = (
        P(("parts", "dp", "fsdp"), "seq", None),
        P(("parts", "dp", "fsdp"), "seq", None),
        P(("parts", "dp", "fsdp"), "seq", None),
        P(("parts", "dp", "fsdp"), "seq", None),
        P(("parts", "dp", "fsdp"), "seq"),
    )
    out_specs = (
        P(("parts", "dp", "fsdp"), "seq", None),
        P(("parts", "dp", "fsdp"), "seq", None),
        P(("parts", "dp", "fsdp"), "seq", None),
        P(("parts", "dp", "fsdp"), "seq", None),
    )
    return jax.shard_map(local, mesh=mesh, in_specs=in_specs, out_specs=out_specs, check_vma=False)
```

profile of v0, /device:TPU:0, one launch (start us, length us, event | category | flops | bytes accessed | tf_op | source)
XLA Modules:
  0.0 134.9 jit_solution(5039545591200088202)
XLA Ops:
  0.6 1.1 copy.68
  2.5 6.3 %all-to-all-start.1 = ((bf16[1,128,4,128]{3,1,0,2:T(8,128)(2,1)}), bf16[1,128,4,128]{3,1,0,2:T(8,128)(2,1)S(1)}, u32[]{:S(2)}, u32[]{:S(2)}) async-start(bf16[1,128,4,128]{3,1,0,2:T(8,128)(2,1)} %copy.69), calls=%async_computation.1 | async-start | bytes 262144 | tf_op jit(solution)/shard_map/all_to_all | solution.py:182
  9.1 1.0 copy.67
  10.1 4.8 %all-to-all-done.1 = bf16[1,128,4,128]{3,1,0,2:T(8,128)(2,1)S(1)} async-done(((bf16[1,128,4,128]{3,1,0,2:T(8,128)(2,1)}), bf16[1,128,4,128]{3,1,0,2:T(8,128)(2,1)S(1)}, u32[]{:S(2)}, u32[]{:S(2)}) %all-to-all-start.1) | async-done | bytes 131104 | tf_op jit(solution)/shard_map/all_to_all | solution.py:182
  14.9 3.5 %all-to-all-start = ((bf16[1,128,4,512]{3,1,0,2:T(8,128)(2,1)}), bf16[1,128,4,512]{3,1,0,2:T(8,128)(2,1)S(1)}, u32[]{:S(2)}, u32[]{:S(2)}) async-start(bf16[1,128,4,512]{3,1,0,2:T(8,128)(2,1)} %copy.67), calls=%async_computation | async-start | bytes 1048576 | tf_op jit(solution)/shard_map/all_to_all | solution.py:181
  18.4 1.0 copy.72
  19.4 12.2 %all-to-all-done = bf16[1,128,4,512]{3,1,0,2:T(8,128)(2,1)S(1)} async-done(((bf16[1,128,4,512]{3,1,0,2:T(8,128)(2,1)}), bf16[1,128,4,512]{3,1,0,2:T(8,128)(2,1)S(1)}, u32[]{:S(2)}, u32[]{:S(2)}) %all-to-all-start) | async-done | bytes 524320 | tf_op jit(solution)/shard_map/all_to_all | solution.py:181
  31.6 3.6 %all-to-all-start.3 = ((bf16[1,128,4,512]{1,3,0,2:T(8,128)(2,1)}), bf16[1,128,4,512]{1,3,0,2:T(8,128)(2,1)S(1)}, u32[]{:S(2)}, u32[]{:S(2)}) async-start(bf16[1,128,4,512]{1,3,0,2:T(8,128)(2,1)} %bitcast.23), calls=%async_computation.3 | async-start | bytes 1048576 | tf_op jit(solution)/shard_map/all_to_all | solution.py:184
  36.1 12.8 %all-to-all-done.3 = bf16[1,128,4,512]{1,3,0,2:T(8,128)(2,1)S(1)} async-done(((bf16[1,128,4,512]{1,3,0,2:T(8,128)(2,1)}), bf16[1,128,4,512]{1,3,0,2:T(8,128)(2,1)S(1)}, u32[]{:S(2)}, u32[]{:S(2)}) %all-to-all-start.3) | async-done | bytes 524320 | tf_op jit(solution)/shard_map/all_to_all | solution.py:184
  48.8 3.3 %all-to-all-start.2 = ((bf16[1,128,4,128]{3,1,0,2:T(8,128)(2,1)}), bf16[1,128,4,128]{3,1,0,2:T(8,128)(2,1)S(1)}, u32[]{:S(2)}, u32[]{:S(2)}) async-start(bf16[1,128,4,128]{3,1,0,2:T(8,128)(2,1)} %copy.71), calls=%async_computation.2 | async-start | bytes 262144 | tf_op jit(solution)/shard_map/all_to_all | solution.py:183
  52.9 11.2 %all_gather.5 = s32[1,512]{1,0:T(1,128)S(1)} all-gather(s32[1,128]{1,0:T(1,128)S(1)} %copy-done.7), channel_id=1, replica_groups=mesh['parts'=2,'seq'=4,'dp'=2,'fsdp'=2] {'seq'}, dimensions={1}, use_global_device_ids=true | all-gather | bytes 2560 | tf_op jit(solution)/shard_map/all_gather | solution.py:186
  66.1 16.5 %while.38 = (s32[]{:T(128)}, bf16[4,512,128]{1,2,0:T(8,128)(2,1)S(1)}, bf16[4,512,128]{1,2,0:T(8,128)(2,1)}, f32[4,512,128]{2,1,0:T(8,128)S(1)}, f32[4,512,128]{...) while((s32[]{:T(128)}, ...), condition=%wide.region_4.5_spmd, body=%wide.region_0.4_spmd.sunk | while | flops 412484608 | bytes 12119701 | solution.py:213
  66.8 1.1 fusion.61
  70.9 1.1 fusion.61
  75.0 1.1 fusion.61
  79.1 1.1 fusion.61
  83.3 1.3 reduce.6
  85.3 3.3 %all-to-all-start.6 = ((bf16[4,2,8192]{2,1,0:T(2,128)(2,1)}), bf16[4,2,8192]{2,1,0:T(2,128)(2,1)S(1)}, u32[]{:S(2)}, u32[]{:S(2)}) async-start(bf16[4,2,8192]{2,1,0:T(2,128)(2,1)} %reshape.187), calls=%async_computation.6 | async-start | bytes 262144 | tf_op jit(solution)/shard_map/all_to_all | solution.py:233
  89.0 1.3 reduce.7
  91.0 3.6 %all-to-all-done.6 = bf16[4,2,8192]{2,1,0:T(2,128)(2,1)S(1)} async-done(((bf16[4,2,8192]{2,1,0:T(2,128)(2,1)}), bf16[4,2,8192]{2,1,0:T(2,128)(2,1)S(1)}, u32[]{:S(2)}, u32[]{:S(2)}) %all-to-all-start.6) | async-done | bytes 131104 | tf_op jit(solution)/shard_map/all_to_all | solution.py:233
  94.6 3.3 %all-to-all-start.7 = ((bf16[4,2,8192]{2,1,0:T(2,128)(2,1)}), bf16[4,2,8192]{2,1,0:T(2,128)(2,1)S(1)}, u32[]{:S(2)}, u32[]{:S(2)}) async-start(bf16[4,2,8192]{2,1,0:T(2,128)(2,1)} %reshape.189), calls=%async_computation.7 | async-start | bytes 262144 | tf_op jit(solution)/shard_map/all_to_all | solution.py:234
  97.9 0.9 copy.79
  98.8 3.7 %reduce.4 = bf16[512,512]{1,0:T(8,128)(2,1)S(1)} reduce(bf16[512,1,1,512]{3,2,1,0:T(2,128)(2,1)S(1)} %bitcast.156, bf16[]{:T(256)} %broadcast.53), dimensions={1,2}, to_apply=%bitcast.101.reduce_sub_computation | reduce | bytes 1048578
  102.5 1.2 reshape.183
  103.8 5.1 %all-to-all-start.4 = ((bf16[4,2,32768]{2,1,0:T(2,128)(2,1)}), bf16[4,2,32768]{2,1,0:T(2,128)(2,1)S(1)}, u32[]{:S(2)}, u32[]{:S(2)}) async-start(bf16[4,2,32768]{2,1,0:T(2,128)(2,1)} %reshape.183), calls=%async_computation.4 | async-start | bytes 1048576 | tf_op jit(solution)/shard_map/all_to_all | solution.py:217
  109.8 3.7 %reduce.5 = bf16[512,512]{1,0:T(8,128)(2,1)S(1)} reduce(bf16[512,1,1,512]{3,2,1,0:T(2,128)(2,1)S(1)} %bitcast.155, bf16[]{:T(256)} %broadcast.53), dimensions={1,2}, to_apply=%bitcast.103.reduce_sub_computation | reduce | bytes 1048578
  113.5 1.2 reshape.185
  114.7 4.5 %all-to-all-done.4 = bf16[4,2,32768]{2,1,0:T(2,128)(2,1)S(1)} async-done(((bf16[4,2,32768]{2,1,0:T(2,128)(2,1)}), bf16[4,2,32768]{2,1,0:T(2,128)(2,1)S(1)}, u32[]{:S(2)}, u32[]{:S(2)}) %all-to-all-start.4) | async-done | bytes 524320 | tf_op jit(solution)/shard_map/all_to_all | solution.py:217
  119.2 3.5 %all-to-all-start.5 = ((bf16[4,2,32768]{2,1,0:T(2,128)(2,1)}), bf16[4,2,32768]{2,1,0:T(2,128)(2,1)S(1)}, u32[]{:S(2)}, u32[]{:S(2)}) async-start(bf16[4,2,32768]{2,1,0:T(2,128)(2,1)} %reshape.185), calls=%async_computation.5 | async-start | bytes 1048576 | tf_op jit(solution)/shard_map/all_to_all | solution.py:224
  125.7 1.0 copy.88
  126.7 6.2 %all-to-all-done.5 = bf16[4,2,32768]{2,1,0:T(2,128)(2,1)S(1)} async-done(((bf16[4,2,32768]{2,1,0:T(2,128)(2,1)}), bf16[4,2,32768]{2,1,0:T(2,128)(2,1)S(1)}, u32[]{:S(2)}, u32[]{:S(2)}) %all-to-all-start.5) | async-done | bytes 524320 | tf_op jit(solution)/shard_map/all_to_all | solution.py:224
  133.8 1.0 copy.89
  (110 shorter events, 23.7 us)
Async XLA Ops:
  0.6 8.2 %copy-start.4 = (bf16[1,128,2048]{2,1,0:T(8,128)(2,1)S(1)}, bf16[1,128,2048]{2,1,0:T(8,128)(2,1)}, u32[]{:S(2)}) copy-start(bf16[1,128,2048]{2,1,0:T(8,128)(2,1)} %param.7) | copy-start | bytes 1572868
  2.5 12.4 %all-to-all-start.1 = ((bf16[1,128,4,128]{3,1,0,2:T(8,128)(2,1)}), bf16[1,128,4,128]{3,1,0,2:T(8,128)(2,1)S(1)}, u32[]{:S(2)}, u32[]{:S(2)}) async-start(bf16[1,128,4,128]{3,1,0,2:T(8,128)(2,1)} %copy.69), calls=%async_computation.1 | async-start | bytes 262144 | tf_op jit(solution)/shard_map/all_to_all | solution.py:182
  10.1 8.3 %copy-start.5 = (bf16[1,128,2048]{2,1,0:T(8,128)(2,1)S(1)}, bf16[1,128,2048]{2,1,0:T(8,128)(2,1)}, u32[]{:S(2)}) copy-start(bf16[1,128,2048]{2,1,0:T(8,128)(2,1)} %param.10) | copy-start | bytes 1572868
  14.9 16.7 %all-to-all-start = ((bf16[1,128,4,512]{3,1,0,2:T(8,128)(2,1)}), bf16[1,128,4,512]{3,1,0,2:T(8,128)(2,1)S(1)}, u32[]{:S(2)}, u32[]{:S(2)}) async-start(bf16[1,128,4,512]{3,1,0,2:T(8,128)(2,1)} %copy.67), calls=%async_computation | async-start | bytes 1048576 | tf_op jit(solution)/shard_map/all_to_all | solution.py:181
  31.6 3.6 %copy-start.6 = (bf16[1,128,512]{2,1,0:T(8,128)(2,1)S(1)}, bf16[1,128,512]{2,1,0:T(8,128)(2,1)}, u32[]{:S(2)}) copy-start(bf16[1,128,512]{2,1,0:T(8,128)(2,1)} %param.9) | copy-start | bytes 393220
  31.6 17.3 %all-to-all-start.3 = ((bf16[1,128,4,512]{1,3,0,2:T(8,128)(2,1)}), bf16[1,128,4,512]{1,3,0,2:T(8,128)(2,1)S(1)}, u32[]{:S(2)}, u32[]{:S(2)}) async-start(bf16[1,128,4,512]{1,3,0,2:T(8,128)(2,1)} %bitcast.23), calls=%async_computation.3 | async-start | bytes 1048576 | tf_op jit(solution)/shard_map/all_to_all | solution.py:184
  48.8 16.2 %all-to-all-start.2 = ((bf16[1,128,4,128]{3,1,0,2:T(8,128)(2,1)}), bf16[1,128,4,128]{3,1,0,2:T(8,128)(2,1)S(1)}, u32[]{:S(2)}, u32[]{:S(2)}) async-start(bf16[1,128,4,128]{3,1,0,2:T(8,128)(2,1)} %copy.71), calls=%async_computation.2 | async-start | bytes 262144 | tf_op jit(solution)/shard_map/all_to_all | solution.py:183
  52.2 0.7 copy-start.7
  65.0 1.0 copy-start.1
  66.7 1.1 copy-start.3
  70.9 1.1 copy-start.3
  75.0 1.1 copy-start.3
  79.1 1.1 copy-start.3
  82.5 6.1 %copy-start = (f32[4,512,128]{2,1,0:T(8,128)S(1)}, f32[4,512,128]{2,1,0:T(8,128)}, u32[]{:S(2)}) copy-start(f32[4,512,128]{2,1,0:T(8,128)} %get-tuple-element.311) | copy-start | bytes 3145732
  85.3 9.2 %all-to-all-start.6 = ((bf16[4,2,8192]{2,1,0:T(2,128)(2,1)}), bf16[4,2,8192]{2,1,0:T(2,128)(2,1)S(1)}, u32[]{:S(2)}, u32[]{:S(2)}) async-start(bf16[4,2,8192]{2,1,0:T(2,128)(2,1)} %reshape.187), calls=%async_computation.6 | async-start | bytes 262144 | tf_op jit(solution)/shard_map/all_to_all | solution.py:233
  94.6 9.2 %all-to-all-start.7 = ((bf16[4,2,8192]{2,1,0:T(2,128)(2,1)}), bf16[4,2,8192]{2,1,0:T(2,128)(2,1)S(1)}, u32[]{:S(2)}, u32[]{:S(2)}) async-start(bf16[4,2,8192]{2,1,0:T(2,128)(2,1)} %reshape.189), calls=%async_computation.7 | async-start | bytes 262144 | tf_op jit(solution)/shard_map/all_to_all | solution.py:234
  103.7 5.2 %copy-start.2 = (bf16[4,512,128]{1,2,0:T(8,128)(2,1)S(1)}, bf16[4,512,128]{1,2,0:T(8,128)(2,1)}, u32[]{:S(2)}) copy-start(bf16[4,512,128]{1,2,0:T(8,128)(2,1)} %get-tuple-element.309) | copy-start | bytes 1572868
  103.8 15.4 %all-to-all-start.4 = ((bf16[4,2,32768]{2,1,0:T(2,128)(2,1)}), bf16[4,2,32768]{2,1,0:T(2,128)(2,1)S(1)}, u32[]{:S(2)}, u32[]{:S(2)}) async-start(bf16[4,2,32768]{2,1,0:T(2,128)(2,1)} %reshape.183), calls=%async_computation.4 | async-start | bytes 1048576 | tf_op jit(solution)/shard_map/all_to_all | solution.py:217
  119.2 13.7 %all-to-all-start.5 = ((bf16[4,2,32768]{2,1,0:T(2,128)(2,1)}), bf16[4,2,32768]{2,1,0:T(2,128)(2,1)S(1)}, u32[]{:S(2)}, u32[]{:S(2)}) async-start(bf16[4,2,32768]{2,1,0:T(2,128)(2,1)} %reshape.185), calls=%async_computation.5 | async-start | bytes 1048576 | tf_op jit(solution)/shard_map/all_to_all | solution.py:224
where the time goes:
time: 136 us; the launch traced here: 135 us
  waiting for transfers between devices  44 us (32%)
  starting transfers between devices  31.9 us (23%)
  local copies, waits for them, and re-layouts  23.1 us (17%)
  other arithmetic  11.7 us (9%)
  matrix products  11.6 us (9%)
  blocking collectives  11.2 us (8%)
    all_to_all x1, waiting for transfers between devices, local(): lax.all_to_all(grad_split, 'seq', split_axis=2, concat_axis=1, tiled=True)  12.8 us
    unnamed x35, local copies, waits for them, and re-layouts  12.6 us
    all_to_all x1, waiting for transfers between devices, local(): lax.all_to_all(query_split, 'seq', split_axis=2, concat_axis=1, tiled=True)  12.2 us
    all_gather x1, blocking collectives, local(): segment_row = lax.all_gather(segments, 'seq', axis=1, tiled=True)  11.2 us
    unnamed x4, other arithmetic  10.1 us
    all_to_all x1, starting transfers between devices, local(): lax.all_to_all(spread_kv(key_states), 'seq', split_axis=2, concat_axis=1,...  6.32 us
    all_to_all x1, waiting for transfers between devices, local(): lax.all_to_all(to_rows(query_grads, local_heads, jnp.bfloat16), 'seq', sp...  6.17 us
    dot_general x8, matrix products, transposed(): lax.dot_general(left, right, (((0,), (0,)), ((), ())), preferred_element_...  5.56 us
  transfers between devices with their start and end apart: 8, of which 7 were waited for; matrix products, arithmetic and copies ran while one was open for 16% of the time, Pallas kernels for 0%

commit v1 on v0

v1 whole, which is shorter than its diff:
```python
import functools

import jax
import jax.numpy as jnp
from jax import lax
from jax.experimental import pallas as pl
from jax.experimental.pallas import tpu as pltpu
from jax.sharding import PartitionSpec as P

H = 16
KVH = 4
HD = 128
RATIO = H // KVH
PAIR = 2
masked_bias = -1e30
MESH = pl.DeviceIdType.MESH


def kernel(
    members,
    reach,
    q_hbm,
    k_hbm,
    v_hbm,
    g_hbm,
    s_hbm,
    o_hbm,
    dq_hbm,
    dk_hbm,
    dv_hbm,
    q_buf,
    g_buf,
    kv_buf,
    o_buf,
    dq_buf,
    own,
    outgoing,
    incoming,
    dkv_buf,
    seg_row,
    seg_buf,
    bias,
    in_sem,
    out_sem,
    seg_sem,
    seg_send,
    seg_recv,
    kv_send,
    kv_recv,
    part_send,
    part_recv,
):
    me = lax.axis_index("seq")
    rows = q_buf.shape[1]
    keys = (reach + 1) * rows
    scale = HD**-0.5
    has_left = me > 0
    has_right = me < members - 1

    def columns(g, width):
        return pl.ds(pl.multiple_of(g * width, width), width)

    def loads(g):
        return (
            pltpu.make_async_copy(k_hbm.at[0, :, columns(g, HD)], kv_buf.at[0, g, 0], in_sem.at[0, g]),
            pltpu.make_async_copy(v_hbm.at[0, :, columns(g, HD)], kv_buf.at[0, g, 1], in_sem.at[1, g]),
            pltpu.make_async_copy(q_hbm.at[0, :, columns(g, RATIO * HD)], q_buf.at[g], in_sem.at[2, g]),
            pltpu.make_async_copy(g_hbm.at[0, :, columns(g, RATIO * HD)], g_buf.at[g], in_sem.at[3, g]),
        )

    def stores(g):
        return (
            pltpu.make_async_copy(o_buf.at[g], o_hbm.at[0, :, columns(g, RATIO * HD)], out_sem.at[0, g]),
            pltpu.make_async_copy(dq_buf.at[g], dq_hbm.at[0, :, columns(g, RATIO * HD)], out_sem.at[1, g]),
            pltpu.make_async_copy(dkv_buf.at[g, 0], dk_hbm.at[0, :, columns(g, HD)], out_sem.at[2, g]),
            pltpu.make_async_copy(dkv_buf.at[g, 1], dv_hbm.at[0, :, columns(g, HD)], out_sem.at[3, g]),
        )

    def kv_copy(w, g):
        return pltpu.make_async_remote_copy(
            src_ref=kv_buf.at[w, g],
            dst_ref=kv_buf.at[w + 1, g],
            send_sem=kv_send.at[w, g],
            recv_sem=kv_recv.at[w, g],
            device_id={"seq": lax.rem(me + 1, members)},
            device_id_type=MESH,
        )

    def seg_copy(w):
        return pltpu.make_async_remote_copy(
            src_ref=seg_buf.at[w],
            dst_ref=seg_buf.at[w + 1],
            send_sem=seg_send.at[w],
            recv_sem=seg_recv.at[w],
            device_id={"seq": lax.rem(me + 1, members)},
            device_id_type=MESH,
        )

    def part_copy(s, g):
        return pltpu.make_async_remote_copy(
            src_ref=outgoing.at[s, g],
            dst_ref=incoming.at[s, g],
            send_sem=part_send.at[s, g],
            recv_sem=part_recv.at[s, g],
            device_id={"seq": lax.rem(me + members - 1, members)},
            device_id_type=MESH,
        )

    seg_load = pltpu.make_async_copy(s_hbm, seg_row, seg_sem)
    seg_load.start()
    for g in range(KVH):
        for copy in loads(g)[:2]:
            copy.start()
    for g in range(KVH):
        for copy in loads(g)[2:]:
            copy.start()

    barrier = pltpu.get_barrier_semaphore()

    @pl.when(has_left)
    def _():
        pl.semaphore_signal(
            barrier, inc=1, device_id={"seq": lax.rem(me + members - 1, members)}, device_id_type=MESH
        )

    @pl.when(has_right)
    def _():
        pl.semaphore_signal(
            barrier, inc=1, device_id={"seq": lax.rem(me + 1, members)}, device_id_type=MESH
        )

    for w in range(1, reach + 1):

        @pl.when(me < w)
        def _(w=w):
            kv_buf[w] = jnp.zeros(kv_buf.shape[1:], kv_buf.dtype)
            seg_buf[w] = jnp.zeros(seg_buf.shape[1:], seg_buf.dtype)

    seg_load.wait()
    seg_buf[0] = jnp.broadcast_to(seg_row[...], seg_buf.shape[1:])
    neighbours = has_left.astype(jnp.int32) + has_right.astype(jnp.int32)
    pl.semaphore_wait(barrier, neighbours)

    def send_own(g):
        for copy in loads(g)[:2]:
            copy.wait()

        @pl.when(has_right)
        def _():
            kv_copy(0, g).start()

    def forward(g):
        for w in range(1, reach):

            @pl.when(me >= w)
            def _(w=w):
                kv_copy(w - 1, g).wait_recv()

                @pl.when(has_right)
                def _():
                    kv_copy(w, g).start()

    @pl.when(has_right)
    def _():
        seg_copy(0).start()

    send_own(0)
    send_own(1)
    for w in range(1, reach + 1):

        @pl.when(me >= w)
        def _(w=w):
            seg_copy(w - 1).wait_recv()
            if w < reach:

                @pl.when(has_right)
                def _():
                    seg_copy(w).start()

    forward(0)

    row_ids = lax.broadcasted_iota(jnp.int32, (rows, rows), 0)
    column_ids = lax.broadcasted_iota(jnp.int32, (rows, rows), 1)
    own_document = jnp.broadcast_to(seg_buf[0, 0:1].astype(jnp.float32), (rows, rows))
    for w in range(reach + 1):
        key_document = jnp.broadcast_to(seg_buf[w, 0:1].astype(jnp.float32), (rows, rows)).T
        allowed = key_document == own_document
        if w == 0:
            allowed = jnp.logical_and(allowed, row_ids <= column_ids)
        block = jnp.where(allowed, 0.0, masked_bias)
        bias[pl.ds(w * rows, rows)] = jnp.where(me >= w, block, masked_bias)

    def contract(left, right):
        return lax.dot_general(left, right, (((1,), (1,)), ((), ())), preferred_element_type=jnp.float32)

    def product(left, right):
        return jnp.dot(left, right, preferred_element_type=jnp.float32)

    def compute(g):
        key = kv_buf[:, g, 0].reshape(keys, HD)
        value = kv_buf[:, g, 1].reshape(keys, HD)
        key_t = key.T
        value_t = value.T
        shift = jnp.concatenate([bias[...]] * PAIR, axis=1)
        key_sum = value_sum = None
        for first in range(0, RATIO, PAIR):
            heads = range(first, first + PAIR)
            query = jnp.concatenate([q_buf[g, :, h * HD : (h + 1) * HD] for h in heads], axis=0)
            grad = jnp.concatenate([g_buf[g, :, h * HD : (h + 1) * HD] for h in heads], axis=0)
            scores = contract(key, query) * scale + shift
            top = jnp.max(scores, axis=0, keepdims=True)
            exponents = jnp.exp(scores - top)
            weights = exponents * (1.0 / jnp.sum(exponents, axis=0, keepdims=True))
            weights_low = weights.astype(jnp.bfloat16)
            spread = contract(value, grad)
            delta = jnp.sum(weights_low.astype(jnp.float32) * spread, axis=0, keepdims=True)
            score_grad = (weights * (spread - delta)).astype(jnp.bfloat16)
            attended = product(value_t, weights_low).T.astype(jnp.bfloat16)
            query_grad = (product(key_t, score_grad) * scale).T.astype(jnp.bfloat16)
            for at, h in enumerate(heads):
                o_buf[g, :, h * HD : (h + 1) * HD] = attended[at * rows : (at + 1) * rows]
                dq_buf[g, :, h * HD : (h + 1) * HD] = query_grad[at * rows : (at + 1) * rows]
            key_part = product(score_grad, query)
            value_part = product(weights_low, grad)
            key_sum = key_part if key_sum is None else key_sum + key_part
            value_sum = value_part if value_sum is None else value_sum + value_part
        key_sum = key_sum * scale
        for w in range(reach + 1):
            block = slice(w * rows, (w + 1) * rows)
            if w < reach:
                own[g, w, 0] = key_sum[block]
                own[g, w, 1] = value_sum[block]
            else:
                outgoing[w - 1, g, 0] = key_sum[block].astype(jnp.bfloat16)
                outgoing[w - 1, g, 1] = value_sum[block].astype(jnp.bfloat16)

    def pass_on(g):
        for w in range(reach - 1, 0, -1):

            @pl.when(me >= w)
            def _(w=w):
                @pl.when(has_right)
                def _():
                    part_copy(w, g).wait_recv()
                    outgoing[w - 1, g] = (own[g, w] + incoming[w, g].astype(jnp.float32)).astype(jnp.bfloat16)

                @pl.when(jnp.logical_not(has_right))
                def _():
                    outgoing[w - 1, g] = own[g, w].astype(jnp.bfloat16)

                part_copy(w - 1, g).start()

    def finish(g):
        @pl.when(has_right)
        def _():
            part_copy(0, g).wait_recv()
            dkv_buf[g] = (own[g, 0] + incoming[0, g].astype(jnp.float32)).astype(jnp.bfloat16)

        @pl.when(jnp.logical_not(has_right))
        def _():
            dkv_buf[g] = own[g, 0].astype(jnp.bfloat16)

        for copy in stores(g)[2:]:
            copy.start()

    def step(g, carry):
        @pl.when(g + 2 < KVH)
        def _():
            send_own(g + 2)

        @pl.when(g + 1 < KVH)
        def _():
            forward(g + 1)

        @pl.when(me >= reach)
        def _():
            kv_copy(reach - 1, g).wait_recv()

        for copy in loads(g)[2:]:
            copy.wait()
        compute(g)

        @pl.when(me >= reach)
        def _():
            part_copy(reach - 1, g).start()

        for copy in stores(g)[:2]:
            copy.start()

        @pl.when(g >= 1)
        def _():
            pass_on(g - 1)

        return carry

    lax.fori_loop(0, KVH, step, 0)
    pass_on(KVH - 1)
    for g in range(KVH):
        finish(g)

    for w in range(reach):

        @pl.when(jnp.logical_and(has_right, me >= w))
        def _(w=w):
            seg_copy(w).wait_send()
            for g in range(KVH):
                kv_copy(w, g).wait_send()

        @pl.when(me >= w + 1)
        def _(w=w):
            for g in range(KVH):
                part_copy(w, g).wait_send()

    for g in range(KVH):
        for copy in stores(g):
            copy.wait()


def local(members, queries, key_states, values, grad_out, segments):
    rows = queries.shape[1]
    reach = max(1, members // 2)
    any_space = pl.BlockSpec(memory_space=pl.ANY)
    low = jnp.bfloat16
    dma = pltpu.SemaphoreType.DMA
    pairs = H * rows * (reach + 1) * rows
    return pl.pallas_call(
        functools.partial(kernel, members, reach),
        out_shape=(
            jax.ShapeDtypeStruct(queries.shape, low),
            jax.ShapeDtypeStruct(queries.shape, low),
            jax.ShapeDtypeStruct(key_states.shape, low),
            jax.ShapeDtypeStruct(values.shape, low),
        ),
        in_specs=[any_space] * 5,
        out_specs=(any_space,) * 4,
        scratch_shapes=[
            pltpu.VMEM((KVH, rows, RATIO * HD), low),
            pltpu.VMEM((KVH, rows, RATIO * HD), low),
            pltpu.VMEM((reach + 1, KVH, 2, rows, HD), low),
            pltpu.VMEM((KVH, rows, RATIO * HD), low),
            pltpu.VMEM((KVH, rows, RATIO * HD), low),
            pltpu.VMEM((KVH, reach, 2, rows, HD), jnp.float32),
            pltpu.VMEM((reach, KVH, 2, rows, HD), low),
            pltpu.VMEM((reach, KVH, 2, rows, HD), low),
            pltpu.VMEM((KVH, 2, rows, HD), low),
            pltpu.VMEM((1, rows), jnp.int32),
            pltpu.VMEM((reach + 1, 8, rows), jnp.int32),
            pltpu.VMEM(((reach + 1) * rows, rows), jnp.float32),
            dma((4, KVH)),
            dma((4, KVH)),
            dma,
            dma((reach,)),
            dma((reach,)),
            dma((reach, KVH)),
            dma((reach, KVH)),
            dma((reach, KVH)),
            dma((reach, KVH)),
        ],
        compiler_params=pltpu.CompilerParams(
            collective_id=0, has_side_effects=True, vmem_limit_bytes=40 * 1024 * 1024
        ),
        cost_estimate=pl.CostEstimate(
            flops=12 * pairs * HD, bytes_accessed=4 * queries.size * 2 + 8 * values.size * 2, transcendentals=pairs
        ),
    )(queries, key_states, values, grad_out, segments)


def solution(mesh):
    spread = ("parts", "dp", "fsdp")
    wide = P(spread, "seq", None)
    return jax.shard_map(
        functools.partial(local, mesh.shape["seq"]),
        mesh=mesh,
        in_specs=(wide, wide, wide, wide, P(spread, "seq")),
        out_specs=(wide, wide, wide, wide),
        check_vma=False,
    )
```

time: 136 us -> 37.2 us (0.27)
  waiting for transfers between devices: 44 us -> 0 us
  starting transfers between devices: 31.9 us -> 0 us
  Pallas kernels: 0 us -> 28.9 us
  local copies, waits for them, and re-layouts: 23.1 us -> 7.44 us
  other arithmetic: 11.7 us -> 0 us
  matrix products: 11.6 us -> 0 us
  blocking collectives: 11.2 us -> 0 us
    all_to_all x8 -> x0, waiting for transfers between devices: 44 us -> none  [the longest x1 12.8 us: local(): lax.all_to_all(grad_split, 'seq', split_axis=2, concat_axis=1, tiled=True)]
    all_to_all x8 -> x0, starting transfers between devices: 31.9 us -> none  [the longest x1 6.32 us: local(): lax.all_to_all(spread_kv(key_states), 'seq', split_axis=2, concat_axis=1,...]
    pallas_call x0 -> x1, Pallas kernels: none -> 28.9 us  [local(): pl.pallas_call(functools.partial(kernel, members, reach), out_shape=(jax....]
    dot_general x24 -> x0, matrix products: 11.6 us -> none  [the longest x8 5.56 us: transposed(): lax.dot_general(left, right, (((0,), (0,)), ((), ())), preferred_element_...]
    all_gather x1 -> x0, blocking collectives: 11.2 us -> none  [local(): segment_row = lax.all_gather(segments, 'seq', axis=1, tiled=True)]
    unnamed x4 -> x0, other arithmetic: 10.1 us -> none
    unnamed x35 -> x14, local copies, waits for them, and re-layouts: 12.6 us -> 7.44 us
    dynamic_update_slice x8 -> x0, local copies, waits for them, and re-layouts: 3.14 us -> none  [local(): lax.map(partial(joined_unit, documents), unit_inputs)]
  transfers between devices with their start and end apart: 8 -> 0, of which waited for: 7 -> 0; matrix products, arithmetic and copies ran while one was open for 16% -> 0% of each run, Pallas kernels for 0% -> 0%
where the time goes in v1:
time: 37.2 us; the launch traced here: 37 us
  Pallas kernels  28.9 us (78%)
  local copies, waits for them, and re-layouts  7.44 us (20%)
  between operations  0.65 us (2%)
    pallas_call x1, Pallas kernels, local(): pl.pallas_call(functools.partial(kernel, members, reach), out_shape=(jax....  28.9 us
    unnamed x14, local copies, waits for them, and re-layouts  7.44 us

profile of v1, /device:TPU:0, one launch (start us, length us, event | category | flops | bytes accessed | tf_op | source)
XLA Modules:
  0.0 37.0 jit_solution(16118025786601341508)
XLA Ops:
  0.6 0.0 copy-start
  0.6 1.0 %copy-done = bf16[1,128,2048]{2,1,0:T(8,128)(2,1)S(1)} copy-done((bf16[1,128,2048]{2,1,0:T(8,128)(2,1)S(1)}, bf16[1,128,2048]{2,1,0:T(8,128)(2,1)}, u32[]{:S(2)}) %copy-start) | copy-done | bytes 524312
  1.7 0.0 copy-start.1
  1.7 1.0 %copy-done.1 = bf16[1,128,2048]{2,1,0:T(8,128)(2,1)S(1)} copy-done((bf16[1,128,2048]{2,1,0:T(8,128)(2,1)S(1)}, bf16[1,128,2048]{2,1,0:T(8,128)(2,1)}, u32[]{:S(2)}) %copy-start.1) | copy-done | bytes 524312
  2.7 0.0 copy-start.2
  2.7 0.9 %copy-done.2 = bf16[1,128,512]{2,1,0:T(8,128)(2,1)S(1)} copy-done((bf16[1,128,512]{2,1,0:T(8,128)(2,1)S(1)}, bf16[1,128,512]{2,1,0:T(8,128)(2,1)}, u32[]{:S(2)}) %copy-start.2) | copy-done | bytes 131096
  3.6 0.0 copy-start.3
  3.6 0.9 %copy-done.3 = bf16[1,128,512]{2,1,0:T(8,128)(2,1)S(1)} copy-done((bf16[1,128,512]{2,1,0:T(8,128)(2,1)S(1)}, bf16[1,128,512]{2,1,0:T(8,128)(2,1)}, u32[]{:S(2)}) %copy-start.3) | copy-done | bytes 131096
  4.5 0.0 copy-start.4
  4.5 0.7 %copy-done.4 = s32[1,128]{1,0:T(1,128)S(1)} copy-done((s32[1,128]{1,0:T(1,128)S(1)}, s32[1,128]{1,0:T(1,128)}, u32[]{:S(2)}) %copy-start.4) | copy-done | bytes 536
  5.2 28.9 %shard_map.84 = (bf16[1,128,2048]{2,1,0:T(8,128)(2,1)S(1)}, bf16[1,128,2048]{2,1,0:T(8,128)(2,1)S(1)}, bf16[1,128,512]{2,1,0:T(8,128)(2,1)S(1)}, bf16[1,128,512]{2,1,0:T(8,128)(2,1)S(1)}) custom-call(bf16[1,128,2048]{2,1,0:T(8,128)(2,1)S(1)} %copy-done, bf16[1,128,512]{2,1,0:T(8,128)(2,1)S(1)} %copy-done.2, bf16[1,128,512]{2,1,0:T(8,128)(2,1)S(1)} %copy-done.3, ...), custom_call_target="tpu_custom_call" | custom-call | flops 1207959552 | bytes 3145728 | tf_op jit(solution)/shard_map/pallas_call | solution.py:326
  34.1 0.8 %copy.13 = bf16[1,128,2048]{2,1,0:T(8,128)(2,1)} copy(bf16[1,128,2048]{2,1,0:T(8,128)(2,1)S(1)} %get-tuple-element.8) | data formatting | bytes 1048576
  34.8 0.8 %copy.14 = bf16[1,128,2048]{2,1,0:T(8,128)(2,1)} copy(bf16[1,128,2048]{2,1,0:T(8,128)(2,1)S(1)} %get-tuple-element.9) | data formatting | bytes 1048576
  35.6 0.7 %copy.15 = bf16[1,128,512]{2,1,0:T(8,128)(2,1)} copy(bf16[1,128,512]{2,1,0:T(8,128)(2,1)S(1)} %get-tuple-element.10) | data formatting | bytes 262144
  36.3 0.7 %copy.16 = bf16[1,128,512]{2,1,0:T(8,128)(2,1)} copy(bf16[1,128,512]{2,1,0:T(8,128)(2,1)S(1)} %get-tuple-element.11) | data formatting | bytes 262144
Async XLA Ops:
  0.6 1.0 %copy-start = (bf16[1,128,2048]{2,1,0:T(8,128)(2,1)S(1)}, bf16[1,128,2048]{2,1,0:T(8,128)(2,1)}, u32[]{:S(2)}) copy-start(bf16[1,128,2048]{2,1,0:T(8,128)(2,1)} %q_hbm.1) | copy-start | bytes 1572868
  1.7 1.0 %copy-start.1 = (bf16[1,128,2048]{2,1,0:T(8,128)(2,1)S(1)}, bf16[1,128,2048]{2,1,0:T(8,128)(2,1)}, u32[]{:S(2)}) copy-start(bf16[1,128,2048]{2,1,0:T(8,128)(2,1)} %g_hbm.1) | copy-start | bytes 1572868
  2.7 0.9 %copy-start.2 = (bf16[1,128,512]{2,1,0:T(8,128)(2,1)S(1)}, bf16[1,128,512]{2,1,0:T(8,128)(2,1)}, u32[]{:S(2)}) copy-start(bf16[1,128,512]{2,1,0:T(8,128)(2,1)} %k_hbm.1) | copy-start | bytes 393220
  3.6 0.9 %copy-start.3 = (bf16[1,128,512]{2,1,0:T(8,128)(2,1)S(1)}, bf16[1,128,512]{2,1,0:T(8,128)(2,1)}, u32[]{:S(2)}) copy-start(bf16[1,128,512]{2,1,0:T(8,128)(2,1)} %v_hbm.1) | copy-start | bytes 393220
  4.5 0.7 %copy-start.4 = (s32[1,128]{1,0:T(1,128)S(1)}, s32[1,128]{1,0:T(1,128)}, u32[]{:S(2)}) copy-start(s32[1,128]{1,0:T(1,128)} %s_hbm.1) | copy-start | bytes 1540

commit v2 on v1

--- a/solution.py
+++ b/solution.py
@@ -60,10 +60,14 @@
     def columns(g, width):
         return pl.ds(pl.multiple_of(g * width, width), width)
 
-    def loads(g):
+    def kv_loads(g):
         return (
             pltpu.make_async_copy(k_hbm.at[0, :, columns(g, HD)], kv_buf.at[0, g, 0], in_sem.at[0, g]),
             pltpu.make_async_copy(v_hbm.at[0, :, columns(g, HD)], kv_buf.at[0, g, 1], in_sem.at[1, g]),
+        )
+
+    def loads(g):
+        return (
             pltpu.make_async_copy(q_hbm.at[0, :, columns(g, RATIO * HD)], q_buf.at[g], in_sem.at[2, g]),
             pltpu.make_async_copy(g_hbm.at[0, :, columns(g, RATIO * HD)], g_buf.at[g], in_sem.at[3, g]),
         )
@@ -72,16 +76,20 @@
         return (
             pltpu.make_async_copy(o_buf.at[g], o_hbm.at[0, :, columns(g, RATIO * HD)], out_sem.at[0, g]),
             pltpu.make_async_copy(dq_buf.at[g], dq_hbm.at[0, :, columns(g, RATIO * HD)], out_sem.at[1, g]),
+        )
+
+    def kv_stores(g):
+        return (
             pltpu.make_async_copy(dkv_buf.at[g, 0], dk_hbm.at[0, :, columns(g, HD)], out_sem.at[2, g]),
             pltpu.make_async_copy(dkv_buf.at[g, 1], dv_hbm.at[0, :, columns(g, HD)], out_sem.at[3, g]),
         )
 
-    def kv_copy(w, g):
+    def kv_copy(w, g, t):
         return pltpu.make_async_remote_copy(
-            src_ref=kv_buf.at[w, g],
-            dst_ref=kv_buf.at[w + 1, g],
-            send_sem=kv_send.at[w, g],
-            recv_sem=kv_recv.at[w, g],
+            src_ref=kv_buf.at[w, g, t],
+            dst_ref=kv_buf.at[w + 1, g, t],
+            send_sem=kv_send.at[w, g, t],
+            recv_sem=kv_recv.at[w, g, t],
             device_id={"seq": lax.rem(me + 1, members)},
             device_id_type=MESH,
         )
@@ -96,12 +104,12 @@
             device_id_type=MESH,
         )
 
-    def part_copy(s, g):
+    def part_copy(s, g, t):
         return pltpu.make_async_remote_copy(
-            src_ref=outgoing.at[s, g],
-            dst_ref=incoming.at[s, g],
-            send_sem=part_send.at[s, g],
-            recv_sem=part_recv.at[s, g],
+            src_ref=outgoing.at[s, g, t],
+            dst_ref=incoming.at[s, g, t],
+            send_sem=part_send.at[s, g, t],
+            recv_sem=part_recv.at[s, g, t],
             device_id={"seq": lax.rem(me + members - 1, members)},
             device_id_type=MESH,
         )
@@ -109,10 +117,10 @@
     seg_load = pltpu.make_async_copy(s_hbm, seg_row, seg_sem)
     seg_load.start()
     for g in range(KVH):
-        for copy in loads(g)[:2]:
+        for copy in kv_loads(g):
             copy.start()
     for g in range(KVH):
-        for copy in loads(g)[2:]:
+        for copy in loads(g):
             copy.start()
 
     barrier = pltpu.get_barrier_semaphore()
@@ -142,23 +150,25 @@
     pl.semaphore_wait(barrier, neighbours)
 
     def send_own(g):
-        for copy in loads(g)[:2]:
+        for copy in kv_loads(g):
             copy.wait()
 
         @pl.when(has_right)
         def _():
-            kv_copy(0, g).start()
+            kv_copy(0, g, 0).start()
+            kv_copy(0, g, 1).start()
 
     def forward(g):
         for w in range(1, reach):
 
             @pl.when(me >= w)
             def _(w=w):
-                kv_copy(w - 1, g).wait_recv()
-
-                @pl.when(has_right)
-                def _():
-                    kv_copy(w, g).start()
+                for t in range(2):
+                    kv_copy(w - 1, g, t).wait_recv()
+
+                    @pl.when(has_right)
+                    def _(t=t):
+                        kv_copy(w, g, t).start()
 
     @pl.when(has_right)
     def _():
@@ -166,6 +176,7 @@
 
     send_own(0)
     send_own(1)
+    forward(0)
     for w in range(1, reach + 1):
 
         @pl.when(me >= w)
@@ -176,8 +187,6 @@
                 @pl.when(has_right)
                 def _():
                     seg_copy(w).start()
-
-    forward(0)
 
     row_ids = lax.broadcasted_iota(jnp.int32, (rows, rows), 0)
     column_ids = lax.broadcasted_iota(jnp.int32, (rows, rows), 1)
@@ -239,28 +248,32 @@
 
             @pl.when(me >= w)
             def _(w=w):
-                @pl.when(has_right)
-                def _():
-                    part_copy(w, g).wait_recv()
-                    outgoing[w - 1, g] = (own[g, w] + incoming[w, g].astype(jnp.float32)).astype(jnp.bfloat16)
-
-                @pl.when(jnp.logical_not(has_right))
-                def _():
-                    outgoing[w - 1, g] = own[g, w].astype(jnp.bfloat16)
-
-                part_copy(w - 1, g).start()
+                for t in (1, 0):
+
+                    @pl.when(has_right)
+                    def _(t=t):
+                        part_copy(w, g, t).wait_recv()
+                        total = own[g, w, t] + incoming[w, g, t].astype(jnp.float32)
+                        outgoing[w - 1, g, t] = total.astype(jnp.bfloat16)
+
+                    @pl.when(jnp.logical_not(has_right))
+                    def _(t=t):
+                        outgoing[w - 1, g, t] = own[g, w, t].astype(jnp.bfloat16)
+
+                    part_copy(w - 1, g, t).start()
 
     def finish(g):
         @pl.when(has_right)
         def _():
-            part_copy(0, g).wait_recv()
+            part_copy(0, g, 1).wait_recv()
+            part_copy(0, g, 0).wait_recv()
             dkv_buf[g] = (own[g, 0] + incoming[0, g].astype(jnp.float32)).astype(jnp.bfloat16)
 
         @pl.when(jnp.logical_not(has_right))
         def _():
             dkv_buf[g] = own[g, 0].astype(jnp.bfloat16)
 
-        for copy in stores(g)[2:]:
+        for copy in kv_stores(g):
             copy.start()
 
     def step(g, carry):
@@ -274,29 +287,35 @@
 
         @pl.when(me >= reach)
         def _():
-            kv_copy(reach - 1, g).wait_recv()
-
-        for copy in loads(g)[2:]:
+            kv_copy(reach - 1, g, 0).wait_recv()
+            kv_copy(reach - 1, g, 1).wait_recv()
+
+        for copy in loads(g):
             copy.wait()
         compute(g)
 
         @pl.when(me >= reach)
         def _():
-            part_copy(reach - 1, g).start()
-
-        for copy in stores(g)[:2]:
+            part_copy(reach - 1, g, 1).start()
+            part_copy(reach - 1, g, 0).start()
+
+        for copy in stores(g):
             copy.start()
 
         @pl.when(g >= 1)
         def _():
             pass_on(g - 1)
+
+        @pl.when(g >= 2)
+        def _():
+            finish(g - 2)
 
         return carry
 
     lax.fori_loop(0, KVH, step, 0)
     pass_on(KVH - 1)
-    for g in range(KVH):
-        finish(g)
+    finish(KVH - 2)
+    finish(KVH - 1)
 
     for w in range(reach):
 
@@ -304,16 +323,40 @@
         def _(w=w):
             seg_copy(w).wait_send()
             for g in range(KVH):
-                kv_copy(w, g).wait_send()
+                kv_copy(w, g, 0).wait_send()
+                kv_copy(w, g, 1).wait_send()
 
         @pl.when(me >= w + 1)
         def _(w=w):
             for g in range(KVH):
-                part_copy(w, g).wait_send()
+                part_copy(w, g, 0).wait_send()
+                part_copy(w, g, 1).wait_send()
 
     for g in range(KVH):
-        for copy in stores(g):
+        for copy in stores(g) + kv_stores(g):
             copy.wait()
+
+
+def place(parts, *refs):
+    sources, results, held, read_sem, write_sem = refs[0:4], refs[4:8], refs[8:12], refs[12], refs[13]
+    pairs = []
+    for i in range(4):
+        size = sources[i].shape[1] // parts
+        for j in range(parts):
+            at = (slice(None), pl.ds(j * size, size))
+            pairs.append(
+                (
+                    pltpu.make_async_copy(sources[i].at[at], held[i].at[at], read_sem.at[i, j]),
+                    pltpu.make_async_copy(held[i].at[at], results[i].at[at], write_sem.at[i, j]),
+                )
+            )
+    for read, _ in pairs:
+        read.start()
+    for read, write in pairs:
+        read.wait()
+        write.start()
+    for _, write in pairs:
+        write.wait()
 
 
 def local(members, queries, key_states, values, grad_out, segments):
@@ -323,7 +366,7 @@
     low = jnp.bfloat16
     dma = pltpu.SemaphoreType.DMA
     pairs = H * rows * (reach + 1) * rows
-    return pl.pallas_call(
+    results = pl.pallas_call(
         functools.partial(kernel, members, reach),
         out_shape=(
             jax.ShapeDtypeStruct(queries.shape, low),
@@ -331,7 +374,7 @@
             jax.ShapeDtypeStruct(key_states.shape, low),
             jax.ShapeDtypeStruct(values.shape, low),
         ),
-        in_specs=[any_space] * 5,
+        in_specs=[pl.BlockSpec(memory_space=pltpu.HBM)] * 5,
         out_specs=(any_space,) * 4,
         scratch_shapes=[
             pltpu.VMEM((KVH, rows, RATIO * HD), low),
@@ -351,18 +394,27 @@
             dma,
             dma((reach,)),
             dma((reach,)),
-            dma((reach, KVH)),
-            dma((reach, KVH)),
-            dma((reach, KVH)),
-            dma((reach, KVH)),
+            dma((reach, KVH, 2)),
+            dma((reach, KVH, 2)),
+            dma((reach, KVH, 2)),
+            dma((reach, KVH, 2)),
         ],
         compiler_params=pltpu.CompilerParams(
-            collective_id=0, has_side_effects=True, vmem_limit_bytes=40 * 1024 * 1024
+            collective_id=0, has_side_effects=True, vmem_limit_bytes=64 * 1024 * 1024
         ),
         cost_estimate=pl.CostEstimate(
             flops=12 * pairs * HD, bytes_accessed=4 * queries.size * 2 + 8 * values.size * 2, transcendentals=pairs
         ),
     )(queries, key_states, values, grad_out, segments)
+    return pl.pallas_call(
+        functools.partial(place, 2),
+        out_shape=tuple(jax.ShapeDtypeStruct(result.shape, result.dtype) for result in results),
+        in_specs=[pl.BlockSpec(memory_space=pltpu.HBM)] * 4,
+        out_specs=(pl.BlockSpec(memory_space=pltpu.HBM),) * 4,
+        scratch_shapes=[pltpu.VMEM(result.shape, result.dtype) for result in results]
+        + [dma((4, 2)), dma((4, 2))],
+        compiler_params=pltpu.CompilerParams(vmem_limit_bytes=64 * 1024 * 1024),
+    )(*results)
 
 
 def solution(mesh):

time: 37.2 us -> 32.5 us (0.87)
  local copies, waits for them, and re-layouts: 7.44 us -> 0 us
  Pallas kernels: 28.9 us -> 31.7 us
    unnamed x14 -> x0, local copies, waits for them, and re-layouts: 7.44 us -> none
    pallas_call x0 -> x1, Pallas kernels: none -> 2.13 us  [local(): pl.pallas_call(functools.partial(place, 2), out_shape=tuple((jax.ShapeDty...]
    pallas_call x1, Pallas kernels: 28.9 us -> 29.6 us  [local(): pl.pallas_call(functools.partial(kernel, members, reach), out_shape=(jax....]
where the time goes in v2:
time: 32.5 us; the launch traced here: 32.4 us
  Pallas kernels  31.7 us (98%)
  between operations  0.64 us (2%)
    pallas_call x1, Pallas kernels, local(): pl.pallas_call(functools.partial(kernel, members, reach), out_shape=(jax....  29.6 us
    pallas_call x1, Pallas kernels, local(): pl.pallas_call(functools.partial(place, 2), out_shape=tuple((jax.ShapeDty...  2.13 us

profile of v2, /device:TPU:0, one launch (start us, length us, event | category | flops | bytes accessed | tf_op | source)
XLA Modules:
  0.0 32.4 jit_solution(808820059479718780)
XLA Ops:
  0.6 29.6 %shard_map.84 = (bf16[1,128,2048]{2,1,0:T(8,128)(2,1)}, bf16[1,128,2048]{2,1,0:T(8,128)(2,1)}, bf16[1,128,512]{2,1,0:T(8,128)(2,1)}, bf16[1,128,512]{2,1,0:T(8,128)(2,1)}) custom-call(bf16[1,128,2048]{2,1,0:T(8,128)(2,1)} %q_hbm.1, bf16[1,128,512]{2,1,0:T(8,128)(2,1)} %k_hbm.1, bf16[1,128,512]{2,1,0:T(8,128)(2,1)} %v_hbm.1, bf16[1,128,2048]{2,1,0:T(8,128)(2,1)} %g_hbm.1, ...), custom_call_target="tpu_custom_call" | custom-call | flops 1207959552 | bytes 3145728 | tf_op jit(solution)/shard_map/pallas_call | solution.py:369
  30.2 2.1 %shard_map.85 = (bf16[1,128,2048]{2,1,0:T(8,128)(2,1)}, bf16[1,128,2048]{2,1,0:T(8,128)(2,1)}, bf16[1,128,512]{2,1,0:T(8,128)(2,1)}, bf16[1,128,512]{2,1,0:T(8,128)(2,1)}) custom-call(bf16[1,128,2048]{2,1,0:T(8,128)(2,1)} %get-tuple-element.8.refs_0_, bf16[1,128,2048]{2,1,0:T(8,128)(2,1)} %get-tuple-element.9.refs_1_, ...), custom_call_target="tpu_custom_call" | custom-call | tf_op jit(solution)/shard_map/pallas_call | solution.py:409

commit v3 on v2

--- a/solution.py
+++ b/solution.py
@@ -86,8 +86,8 @@
 
     def kv_copy(w, g, t):
         return pltpu.make_async_remote_copy(
-            src_ref=kv_buf.at[w, g, t],
-            dst_ref=kv_buf.at[w + 1, g, t],
+            src_ref=kv_buf.at[w, g],
+            dst_ref=kv_buf.at[w + 1, g],
             send_sem=kv_send.at[w, g, t],
             recv_sem=kv_recv.at[w, g, t],
             device_id={"seq": lax.rem(me + 1, members)},
@@ -156,14 +156,13 @@
         @pl.when(has_right)
         def _():
             kv_copy(0, g, 0).start()
-            kv_copy(0, g, 1).start()
 
     def forward(g):
         for w in range(1, reach):
 
             @pl.when(me >= w)
             def _(w=w):
-                for t in range(2):
+                for t in range(1):
                     kv_copy(w - 1, g, t).wait_recv()
 
                     @pl.when(has_right)
@@ -288,7 +287,6 @@
         @pl.when(me >= reach)
         def _():
             kv_copy(reach - 1, g, 0).wait_recv()
-            kv_copy(reach - 1, g, 1).wait_recv()
 
         for copy in loads(g):
             copy.wait()
@@ -302,20 +300,17 @@
         for copy in stores(g):
             copy.start()
 
-        @pl.when(g >= 1)
-        def _():
-            pass_on(g - 1)
-
         @pl.when(g >= 2)
         def _():
-            finish(g - 2)
+            pass_on(g - 2)
 
         return carry
 
     lax.fori_loop(0, KVH, step, 0)
+    pass_on(KVH - 2)
     pass_on(KVH - 1)
-    finish(KVH - 2)
-    finish(KVH - 1)
+    for g in range(KVH):
+        finish(g)
 
     for w in range(reach):
 
@@ -324,7 +319,6 @@
             seg_copy(w).wait_send()
             for g in range(KVH):
                 kv_copy(w, g, 0).wait_send()
-                kv_copy(w, g, 1).wait_send()
 
         @pl.when(me >= w + 1)
         def _(w=w):

time: 32.5 us -> 31 us (0.954)
  Pallas kernels: 31.7 us -> 30.2 us
    pallas_call x1, Pallas kernels: 29.6 us -> 28.1 us  [local(): pl.pallas_call(functools.partial(kernel, members, reach), out_shape=(jax....]
where the time goes in v3:
time: 31 us; the launch traced here: 30.8 us
  Pallas kernels  30.2 us (97%)
  between operations  0.64 us (2%)
    pallas_call x1, Pallas kernels, local(): pl.pallas_call(functools.partial(kernel, members, reach), out_shape=(jax....  28.1 us
    pallas_call x1, Pallas kernels, local(): pl.pallas_call(functools.partial(place, 2), out_shape=tuple((jax.ShapeDty...  2.13 us

profile of v3, /device:TPU:0, one launch (start us, length us, event | category | flops | bytes accessed | tf_op | source)
XLA Modules:
  0.0 30.8 jit_solution(3261816419696172777)
XLA Ops:
  0.6 28.1 %shard_map.84 = (bf16[1,128,2048]{2,1,0:T(8,128)(2,1)}, bf16[1,128,2048]{2,1,0:T(8,128)(2,1)}, bf16[1,128,512]{2,1,0:T(8,128)(2,1)}, bf16[1,128,512]{2,1,0:T(8,128)(2,1)}) custom-call(bf16[1,128,2048]{2,1,0:T(8,128)(2,1)} %q_hbm.1, bf16[1,128,512]{2,1,0:T(8,128)(2,1)} %k_hbm.1, bf16[1,128,512]{2,1,0:T(8,128)(2,1)} %v_hbm.1, bf16[1,128,2048]{2,1,0:T(8,128)(2,1)} %g_hbm.1, ...), custom_call_target="tpu_custom_call" | custom-call | flops 1207959552 | bytes 3145728 | tf_op jit(solution)/shard_map/pallas_call | solution.py:363
  28.7 2.1 %shard_map.85 = (bf16[1,128,2048]{2,1,0:T(8,128)(2,1)}, bf16[1,128,2048]{2,1,0:T(8,128)(2,1)}, bf16[1,128,512]{2,1,0:T(8,128)(2,1)}, bf16[1,128,512]{2,1,0:T(8,128)(2,1)}) custom-call(bf16[1,128,2048]{2,1,0:T(8,128)(2,1)} %get-tuple-element.8.refs_0_, bf16[1,128,2048]{2,1,0:T(8,128)(2,1)} %get-tuple-element.9.refs_1_, ...), custom_call_target="tpu_custom_call" | custom-call | tf_op jit(solution)/shard_map/pallas_call | solution.py:403

commit v4 on v3

--- a/solution.py
+++ b/solution.py
@@ -174,8 +174,8 @@
         seg_copy(0).start()
 
     send_own(0)
+    forward(0)
     send_own(1)
-    forward(0)
     for w in range(1, reach + 1):
 
         @pl.when(me >= w)

time: 31 us -> 31.1 us (level)
  no operation moved by 1% of the time
where the time goes in v4:
time: 31.1 us; the launch traced here: 30.9 us
  Pallas kernels  30.3 us (97%)
  between operations  0.64 us (2%)
    pallas_call x1, Pallas kernels, local(): pl.pallas_call(functools.partial(kernel, members, reach), out_shape=(jax....  28.1 us
    pallas_call x1, Pallas kernels, local(): pl.pallas_call(functools.partial(place, 2), out_shape=tuple((jax.ShapeDty...  2.13 us

profile of v4, /device:TPU:0, one launch (start us, length us, event | category | flops | bytes accessed | tf_op | source)
XLA Modules:
  0.0 30.9 jit_solution(10663222654376430948)
XLA Ops:
  0.6 28.1 %shard_map.84 = (bf16[1,128,2048]{2,1,0:T(8,128)(2,1)}, bf16[1,128,2048]{2,1,0:T(8,128)(2,1)}, bf16[1,128,512]{2,1,0:T(8,128)(2,1)}, bf16[1,128,512]{2,1,0:T(8,128)(2,1)}) custom-call(bf16[1,128,2048]{2,1,0:T(8,128)(2,1)} %q_hbm.1, bf16[1,128,512]{2,1,0:T(8,128)(2,1)} %k_hbm.1, bf16[1,128,512]{2,1,0:T(8,128)(2,1)} %v_hbm.1, bf16[1,128,2048]{2,1,0:T(8,128)(2,1)} %g_hbm.1, ...), custom_call_target="tpu_custom_call" | custom-call | flops 1207959552 | bytes 3145728 | tf_op jit(solution)/shard_map/pallas_call | solution.py:363
  28.8 2.1 %shard_map.85 = (bf16[1,128,2048]{2,1,0:T(8,128)(2,1)}, bf16[1,128,2048]{2,1,0:T(8,128)(2,1)}, bf16[1,128,512]{2,1,0:T(8,128)(2,1)}, bf16[1,128,512]{2,1,0:T(8,128)(2,1)}) custom-call(bf16[1,128,2048]{2,1,0:T(8,128)(2,1)} %get-tuple-element.8.refs_0_, bf16[1,128,2048]{2,1,0:T(8,128)(2,1)} %get-tuple-element.9.refs_1_, ...), custom_call_target="tpu_custom_call" | custom-call | tf_op jit(solution)/shard_map/pallas_call | solution.py:403
